TPU v7x, 32 devices: a whole 2x2x4 slice. The times are simulated.
32 devices in a mesh: groups: 2 (over y), block: 16 (over z, x, core).
Axes of the slice: x: 2, y: 2, z: 4, core: 2. Of those that a mesh axis runs over, the one named last changes fastest.
Arguments:
- tokens: bfloat16 [4096, 2048], P(('groups', 'block')), parts along dimension 0, may hold values from -6 to 6
- expert_ids: int32 [4096, 8], P(('groups', 'block')), parts along dimension 0, may hold values from 0 to 15, all different within a row; in each aligned block of 128 rows (0 to 127, 128 to 255, ...) at most 96 rows name the same one
- route_weight: float32 [4096, 8], P(('groups', 'block')), parts along dimension 0, may hold values from 0.1 to 1
- memory_keep: float32 [32, 2048], P(('groups', 'block')), parts along dimension 0, may hold values from 0 to 1
- mem_keys: bfloat16 [32, 2048], replicated, may hold values from -4 to 4
- w_gate: bfloat16 [16, 2048, 768], P('block'), may hold values from -0.125 to 0.125
- w_up: bfloat16 [16, 2048, 768], P('block'), may hold values from -0.125 to 0.125
- w_down: bfloat16 [16, 768, 2048], P('block'), may hold values from -0.21875 to 0.21875
Outputs:
- mixed: bfloat16 [4096, 2048], P(('groups', 'block')), parts along dimension 0
- memory_state: float32 [1024, 2048], P(('groups', 'block')), parts along dimension 0
There are 2 independent parts, one for each index of `groups`. A program takes and returns all parts, laid end to end along the dimension named above; an argument that names none is the same for every part. Nothing has to cross between parts.
Inputs may be any that keep to these rules, and one draw needn't show every extreme that they name: `expert_ids`: in each aligned block of 128 rows (the rows of one clip) no expert is named by more than 96 rows; a row names 8 different experts.
All inputs are finite; a program needn't handle non-finite values.
Results may differ from a plain program's by a relative error of at most 0.0058.
Values may be sent and summed in bfloat16 or wider, within the bound.
A program may use at most 192 MiB of HBM per device.

v0:
```python
import functools

import jax
import jax.numpy as jnp
from jax import lax
from jax.experimental import pallas as pl
from jax.experimental.pallas import tpu as pltpu
from jax.sharding import PartitionSpec as P


def prefix(value, axis, join, neutral):
    count, mine = (lax.axis_size(axis), lax.axis_index(axis))
    pieces = jax.tree.map(lambda part: lax.all_gather(part, axis), value)
    subtotal = jax.tree.map(
        lambda part, zero: jnp.full_like(part, 0) + jnp.asarray(zero, part.dtype), value, neutral
    )

    def lap(position, subtotal):
        longer = join(subtotal, jax.tree.map(lambda part: part[position], pieces))
        return jax.tree.map(lambda new, old: jnp.where(position < mine, new, old), longer, subtotal)

    return lax.fori_loop(0, count - 1, lap, subtotal)


def run_expert(received, gate_w, up_w, down_w):
    count, slots, width = received.shape
    flat = received.reshape(count * slots, width)
    gate = jnp.dot(flat, gate_w, preferred_element_type=jnp.float32)
    upper = jnp.dot(flat, up_w, preferred_element_type=jnp.float32)
    hidden = (jax.nn.silu(gate) * upper).astype(jnp.bfloat16)
    produced = jnp.dot(hidden, down_w, preferred_element_type=jnp.float32).astype(jnp.bfloat16)
    return produced.reshape(count, slots, width)


def chain(earlier, later):
    return (earlier[0] * later[0], later[0][None, :] * earlier[1] + later[1])


def sparse_moe(tokens, expert_ids, route_weight, w_gate, w_up, w_down):
    tok_rows, width = tokens.shape
    topk = expert_ids.shape[1]
    experts = lax.axis_size("block")
    capacity = max(2, (3 * tok_rows * topk + 2 * experts - 1) // (2 * experts))
    pairs = expert_ids.reshape(-1)
    onehot = (pairs[:, None] == jnp.arange(experts, dtype=jnp.int32)[None, :]).astype(jnp.int32)
    slot = jnp.sum((jnp.cumsum(onehot, axis=0) - onehot) * onehot, axis=1)
    dest = pairs * capacity + slot
    source_rows = jnp.repeat(tokens, topk, axis=0)
    outgoing = jnp.zeros((experts * capacity, width), jnp.bfloat16).at[dest].set(source_rows)
    outgoing = outgoing.reshape(experts, capacity, width)
    received = lax.all_to_all(outgoing, "block", split_axis=0, concat_axis=0, tiled=True)
    produced = run_expert(received, w_gate[0], w_up[0], w_down[0])
    returned = lax.all_to_all(produced, "block", split_axis=0, concat_axis=0, tiled=True)
    picked = returned.reshape(experts * capacity, width)[dest]
    weighted = picked.astype(jnp.float32).reshape(tok_rows, topk, width) * route_weight[:, :, None]
    return jnp.sum(weighted, axis=1)


def sparse(tokens, expert_ids, route_weight, memory_keep, mem_keys, w_gate, w_up, w_down):
    tok_rows, width = tokens.shape
    moe = sparse_moe(tokens, expert_ids, route_weight, w_gate, w_up, w_down)
    scale_d = width ** (-0.5)
    scores = (jnp.dot(tokens, mem_keys.T, preferred_element_type=jnp.float32) * scale_d).astype(
        jnp.bfloat16
    )
    write = jnp.dot(scores.T, tokens, preferred_element_type=jnp.float32) / tok_rows
    survival_flags = memory_keep[0]
    identity = (jnp.ones_like(survival_flags), jnp.zeros_like(write))
    _, memory_in = prefix((survival_flags, write), "block", chain, identity)
    memory_state = survival_flags[None, :] * memory_in + write
    return finish(tokens, moe, memory_in), memory_state


def finish(tokens, moe, memory_in):
    scale_d = tokens.shape[1] ** (-0.5)
    scale_m = memory_in.shape[0] ** (-0.5)
    memory_read = memory_in.astype(jnp.bfloat16)
    read_scores = (
        jnp.dot(tokens, memory_read.T, preferred_element_type=jnp.float32) * scale_d
    ).astype(jnp.bfloat16)
    recall = jnp.dot(read_scores, memory_read, preferred_element_type=jnp.float32) * scale_m
    return (moe.astype(jnp.float32) + recall).astype(jnp.bfloat16)


def dot(a, b, ca=1, cb=0):
    return lax.dot_general(a, b, (((ca,), (cb,)), ((), ())), preferred_element_type=jnp.float32)


def dense_kernel(
    count,
    tokens_ref,
    aux_ref,
    keys_ref,
    gate_ref,
    up_ref,
    down_ref,
    mixed_ref,
    state_ref,
    clips,
    aux,
    gate_w,
    up_w,
    down_w,
    kept,
    given,
    taken,
    landed,
    writes,
    base,
    load_sem,
    ring_send,
    ring_recv,
    twin_send,
    twin_recv,
    given_send,
    taken_recv,
    sum_send,
    sum_recv,
):
    turn = count // 2
    line = turn // 2
    half = turn // 2
    rows, width = tokens_ref.shape
    hidden_width = gate_w.shape[1]
    mem = keys_ref.shape[0]
    me = lax.axis_index("block")
    core = lax.rem(me, 2)
    my_x = lax.rem(me // 2, 2)
    my_z = me // 4
    here = my_x * (2 * line - 1 - my_z) + (1 - my_x) * my_z
    way = 1 - 2 * core

    def block_of(place, on):
        x = place // line
        z = x * (2 * line - 1 - place) + (1 - x) * place
        return (z * 2 + x) * 2 + on

    def wrap(value):
        return lax.rem(value + 2 * turn, turn)

    ahead = block_of(wrap(here + way), core)
    behind = block_of(wrap(here - way), core)
    twin = block_of(here, 1 - core)

    def remote(src, dst, send, recv, to):
        return pltpu.make_async_remote_copy(
            src_ref=src,
            dst_ref=dst,
            send_sem=send,
            recv_sem=recv,
            device_id={"block": to},
            device_id_type=pl.DeviceIdType.MESH,
        )

    def offset(n):
        odd = lax.rem(n, 2)
        return wrap((1 - 2 * odd) * ((n + 1) // 2) * way)

    def hop(n, place, to):
        return [
            remote(buf.at[place, core], buf.at[place, core], ring_send.at[i, n], ring_recv.at[i, n], to)
            for i, buf in enumerate((clips, aux))
        ]

    def swap(off, on):
        place = wrap(here + off)
        return [
            remote(buf.at[place, on], buf.at[place, on], twin_send.at[i, off], twin_recv.at[i, off], twin)
            for i, buf in enumerate((clips, aux))
        ]

    def pass_part(off):
        return remote(given.at[off], taken.at[off], given_send.at[off], taken_recv.at[off], twin)

    def pass_sum(i, off, to):
        return remote(kept.at[off], landed.at[i], sum_send.at[i], sum_recv.at[i], to)

    def start(copies):
        for copy in copies:
            copy.start()

    loads = [
        pltpu.make_async_copy(tokens_ref, clips.at[here, core], load_sem.at[0]),
        pltpu.make_async_copy(aux_ref, aux.at[here, core], load_sem.at[1]),
        pltpu.make_async_copy(gate_ref.at[0], gate_w, load_sem.at[2]),
        pltpu.make_async_copy(up_ref.at[0], up_w, load_sem.at[3]),
        pltpu.make_async_copy(down_ref.at[0], down_w, load_sem.at[4]),
    ]
    start(loads)

    barrier = pltpu.get_barrier_semaphore()
    for other in (ahead, behind, twin):
        pl.semaphore_signal(
            barrier, inc=1, device_id={"block": other}, device_id_type=pl.DeviceIdType.MESH
        )
    pl.semaphore_wait(barrier, 3)

    loads[0].wait()
    loads[1].wait()
    start(hop(1, here, ahead))
    start(hop(2, here, behind))
    start(swap(0, core))
    for load in loads[2:]:
        load.wait()

    scale_d = width ** (-0.5)
    scale_m = mem ** (-0.5)
    eye = lax.broadcasted_iota(jnp.int32, (rows, rows), 0) == lax.broadcasted_iota(
        jnp.int32, (rows, rows), 1
    )

    def column(place, on):
        row = aux[place, on, pl.ds(me, 1), :]
        return jnp.sum(jnp.where(eye, jnp.broadcast_to(row, (rows, rows)), 0.0), axis=1, keepdims=True)

    def work(off):
        place = wrap(here + off)
        x = clips[place].reshape(2 * rows, width)
        hidden = []
        for at in range(0, hidden_width, 256):
            cols = slice(at, min(at + 256, hidden_width))
            g = dot(x, gate_w[:, cols])
            u = dot(x, up_w[:, cols])
            hidden.append((g / (1.0 + jnp.exp(-g)) * u).astype(jnp.bfloat16))
        hidden = jnp.concatenate(hidden, axis=1)
        shares = jnp.concatenate([column(place, 0), column(place, 1)], axis=0)
        for at in range(0, width, 512):
            cols = slice(at, min(at + 512, width))
            out = (dot(hidden, down_w[:, cols]) * shares).astype(jnp.bfloat16)
            out = out.reshape(2, rows, out.shape[1])

            @pl.when(core == 0)
            def _():
                kept[off, :, cols] = out[0]
                given[off, :, cols] = out[1]

            @pl.when(core == 1)
            def _():
                kept[off, :, cols] = out[1]
                given[off, :, cols] = out[0]

        pass_part(off).start()
        scores = (dot(x, keys_ref[...], 1, 1) * scale_d).astype(jnp.bfloat16)
        for on in range(2):
            piece = slice(on * rows, (on + 1) * rows)
            writes[block_of(place, on)] = dot(scores[piece], x[piece], 0, 0) * (1.0 / rows)

    def add_up(off, parts):
        pass_part(off).wait_recv()

        def some(i, _):
            at = pl.ds(pl.multiple_of(i * 16, 16), 16)
            total = kept[off, at, :].astype(jnp.float32) + taken[off, at, :].astype(jnp.float32)
            for part in parts:
                total = total + landed[part, at, :].astype(jnp.float32)
            kept[off, at, :] = total.astype(jnp.bfloat16)
            return 0

        lax.fori_loop(0, rows // 16, some, 0)

    def long_sum(i):
        off = wrap((half - i) * way)
        if i > 0:
            pass_sum(i - 1, off, ahead).wait_recv()
        add_up(off, [i - 1] if i > 0 else [])
        pass_sum(i, off, ahead).start()

    def short_sum(i):
        off = wrap((i - (half - 1)) * way)
        if i > 0:
            pass_sum(half + i - 1, off, behind).wait_recv()
        add_up(off, [half + i - 1] if i > 0 else [])
        pass_sum(half + i, off, behind).start()

    def arrive(n, to):
        off = offset(n)
        place = wrap(here + off)
        for copy in hop(n, place, to):
            copy.wait_recv()

        @pl.when(n + 2 <= turn - 1)
        def _():
            start(hop(n + 2, place, to))

        start(swap(off, core))

    def step(n, _):
        off = offset(n)

        @pl.when(lax.rem(n, 2) == 1)
        def _():
            arrive(n, ahead)

            @pl.when(n + 1 <= turn - 2)
            def _():
                arrive(n + 1, behind)

        for copy in swap(off, 1 - core):
            copy.wait_recv()
        work(off)

        @pl.when(n == turn - 2)
        def _():
            short_sum(0)

        return 0

    lax.fori_loop(0, turn, step, 0)
    long_sum(0)

    def lap(clip, carry):
        place_x = lax.rem(clip // 2, 2)
        place_z = clip // 4
        place = place_x * (2 * line - 1 - place_z) + (1 - place_x) * place_z
        keep = keep_row(aux[place, lax.rem(clip, 2), count:, :])
        longer = keep * state_ref[...] + writes[clip]
        state_ref[...] = longer
        return carry

    def keep_row(block):
        return jnp.concatenate([block[i : i + 1, :] for i in range(block.shape[0])], axis=1)

    state_ref[...] = jnp.zeros((mem, width), jnp.float32)
    lax.fori_loop(0, me, lap, 0)
    read = state_ref[...].astype(jnp.bfloat16)
    lap(me, 0)
    own = clips[here, core]
    scores = (dot(own, read, 1, 1) * scale_d).astype(jnp.bfloat16)
    for at in range(0, width, 512):
        cols = slice(at, min(at + 512, width))
        base[:, cols] = dot(scores, read[:, cols]) * scale_m

    for i in range(1, half):
        if i < half - 1:
            short_sum(i)
        long_sum(i)

    pass_part(0).wait_recv()
    pass_sum(half - 1, 0, ahead).wait_recv()
    pass_sum(2 * half - 2, 0, behind).wait_recv()

    def finish_some(i, _):
        at = pl.ds(pl.multiple_of(i * 16, 16), 16)
        total = kept[0, at, :].astype(jnp.float32) + taken[0, at, :].astype(jnp.float32)
        total = total + landed[half - 1, at, :].astype(jnp.float32)
        total = total + landed[2 * half - 2, at, :].astype(jnp.float32)
        mixed_ref[at, :] = (total + base[at, :]).astype(jnp.bfloat16)
        return 0

    lax.fori_loop(0, rows // 16, finish_some, 0)

    for n in range(1, turn):
        for copy in hop(n, here, ahead):
            copy.wait_send()
    for off in range(turn):
        for copy in swap(off, core):
            copy.wait_send()
        pass_part(off).wait_send()
    for i in range(2 * half - 1):
        pass_sum(i, 0, ahead).wait_send()


def dense(tokens, expert_ids, route_weight, memory_keep, mem_keys, w_gate, w_up, w_down):
    rows, width = tokens.shape
    mem = mem_keys.shape[0]
    hidden = w_gate.shape[2]
    count = lax.axis_size("block")
    turn = count // 2
    hot = expert_ids[None, :, :] == jnp.arange(count, dtype=jnp.int32)[:, None, None]
    shares = jnp.sum(jnp.where(hot, route_weight[None, :, :], 0.0), axis=2)
    aux = jnp.concatenate([shares, memory_keep.reshape(-1, rows)], axis=0)
    bf16, f32 = jnp.bfloat16, jnp.float32
    anywhere = pl.BlockSpec(memory_space=pl.ANY)
    vmem = pl.BlockSpec(memory_space=pltpu.VMEM)
    dma = pltpu.SemaphoreType.DMA
    return pl.pallas_call(
        functools.partial(dense_kernel, count),
        out_shape=(
            jax.ShapeDtypeStruct((rows, width), bf16),
            jax.ShapeDtypeStruct((mem, width), f32),
        ),
        in_specs=[anywhere, anywhere, vmem, anywhere, anywhere, anywhere],
        out_specs=(vmem, vmem),
        scratch_shapes=[
            pltpu.VMEM((turn, 2, rows, width), bf16),
            pltpu.VMEM((turn, 2) + aux.shape, f32),
            pltpu.VMEM((width, hidden), bf16),
            pltpu.VMEM((width, hidden), bf16),
            pltpu.VMEM((hidden, width), bf16),
            pltpu.VMEM((turn, rows, width), bf16),
            pltpu.VMEM((turn, rows, width), bf16),
            pltpu.VMEM((turn, rows, width), bf16),
            pltpu.VMEM((turn - 1, rows, width), bf16),
            pltpu.VMEM((count, mem, width), f32),
            pltpu.VMEM((rows, width), f32),
            dma((5,)),
            dma((2, turn)),
            dma((2, turn)),
            dma((2, turn)),
            dma((2, turn)),
            dma((turn,)),
            dma((turn,)),
            dma((turn - 1,)),
            dma((turn - 1,)),
        ],
        compiler_params=pltpu.CompilerParams(
            collective_id=0, has_side_effects=True, vmem_limit_bytes=56 * 2**20
        ),
        cost_estimate=pl.CostEstimate(
            flops=6 * count * rows * width * hidden, bytes_accessed=2 * 3 * width * hidden, transcendentals=0
        ),
    )(tokens, aux, mem_keys, w_gate, w_up, w_down)


def solution(mesh):
    experts = mesh.shape["block"]

    def shards(tokens, expert_ids, *rest):
        few = experts <= 4 * expert_ids.shape[1]
        return (dense if few else sparse)(tokens, expert_ids, *rest)

    return jax.shard_map(
        shards,
        mesh=mesh,
        in_specs=(
            P(("groups", "block"), None),
            P(("groups", "block"), None),
            P(("groups", "block"), None),
            P(("groups", "block"), None),
            P(),
            P("block", None, None),
            P("block", None, None),
            P("block", None, None),
        ),
        out_specs=(P(("groups", "block"), None), P(("groups", "block"), None)),
        check_vma=False,
    )
```

profile of v0, /device:TPU:0, one launch (start us, length us, event | category | flops | bytes accessed | tf_op | source)
XLA Modules:
  0.0 114.9 jit_solution(8570089200030080446)
XLA Ops:
  0.6 0.7 select_reduce_fusion
  1.4 1.3 %pad_maximum_fusion.aux_ref = f32[32,128]{1,0:T(8,128)} fusion(f32[16,128]{1,0:T(8,128)} %bitcast.1, f32[16,128]{1,0:T(8,128)S(1)} %select_reduce_fusion), kind=kLoop, calls=%fused_computation.2 | loop fusion | flops 4096 | bytes 32768 | tf_op jit(solution)/shard_map/concatenate | solution.py:371
  2.7 108.7 %shard_map.95 = (bf16[128,2048]{1,0:T(8,128)(2,1)}, f32[32,2048]{1,0:T(8,128)}) custom-call(bf16[128,2048]{1,0:T(8,128)(2,1)} %tokens_ref.1, f32[32,128]{1,0:T(8,128)} %pad_maximum_fusion.aux_ref, bf16[32,2048]{1,0:T(8,128)(2,1)} %keys_ref.1, bf16[1,2048,768]{2,1,0:T(8,128)(2,1)} %gate_ref.1, bf16[1,2048,768]{2,1,0:T(8,128)(2,1)} %up_ref.1, ...), custom_call_target="tpu_custom_call" | custom-call | flops 19327352832 | bytes 9437184 | tf_op jit(solution)/shard_map/pallas_call | solution.py:376
  111.3 1.9 %copy.14 = bf16[128,2048]{1,0:T(8,128)(2,1)} copy(bf16[128,2048]{1,0:T(8,128)(2,1)} %get-tuple-element.4) | data formatting | bytes 1048576
  113.2 1.7 %copy.15 = f32[32,2048]{1,0:T(8,128)} copy(f32[32,2048]{1,0:T(8,128)} %get-tuple-element.5) | data formatting | bytes 524288
where the time goes:
time: 115 us
  Pallas kernels  109 us (95%)
  local copies, waits for them, and re-layouts  3.55 us (3%)
  other arithmetic  2.03 us (2%)
    pallas_call x1, Pallas kernels, dense(): pl.pallas_call(functools.partial(dense_kernel, count), out_shape=(jax.Sha...  109 us
    unnamed x2, local copies, waits for them, and re-layouts  3.55 us

commit v1 on v0

--- a/solution.py
+++ b/solution.py
@@ -101,34 +101,35 @@
     gate_w,
     up_w,
     down_w,
-    kept,
-    given,
+    parts,
     taken,
     landed,
-    writes,
     base,
     load_sem,
     ring_send,
     ring_recv,
     twin_send,
     twin_recv,
-    given_send,
-    taken_recv,
+    part_send,
+    part_recv,
     sum_send,
     sum_recv,
 ):
     turn = count // 2
     line = turn // 2
-    half = turn // 2
+    far = turn // 2
     rows, width = tokens_ref.shape
+    piece = rows // 2
     hidden_width = gate_w.shape[1]
     mem = keys_ref.shape[0]
     me = lax.axis_index("block")
     core = lax.rem(me, 2)
-    my_x = lax.rem(me // 2, 2)
-    my_z = me // 4
-    here = my_x * (2 * line - 1 - my_z) + (1 - my_x) * my_z
     way = 1 - 2 * core
+
+    def place_of(block):
+        x = lax.rem(block // 2, 2)
+        z = block // 4
+        return x * (2 * line - 1 - z) + (1 - x) * z
 
     def block_of(place, on):
         x = place // line
@@ -138,9 +139,15 @@
     def wrap(value):
         return lax.rem(value + 2 * turn, turn)
 
+    here = place_of(me)
     ahead = block_of(wrap(here + way), core)
     behind = block_of(wrap(here - way), core)
     twin = block_of(here, 1 - core)
+
+    def span(h):
+        if isinstance(h, int):
+            return pl.ds(h * piece, piece)
+        return pl.ds(pl.multiple_of(h * piece, piece), piece)
 
     def remote(src, dst, send, recv, to):
         return pltpu.make_async_remote_copy(
@@ -156,28 +163,43 @@
         odd = lax.rem(n, 2)
         return wrap((1 - 2 * odd) * ((n + 1) // 2) * way)
 
-    def hop(n, place, to):
-        return [
-            remote(buf.at[place, core], buf.at[place, core], ring_send.at[i, n], ring_recv.at[i, n], to)
-            for i, buf in enumerate((clips, aux))
-        ]
-
-    def swap(off, on):
-        place = wrap(here + off)
-        return [
-            remote(buf.at[place, on], buf.at[place, on], twin_send.at[i, off], twin_recv.at[i, off], twin)
-            for i, buf in enumerate((clips, aux))
-        ]
-
-    def pass_part(off):
-        return remote(given.at[off], taken.at[off], given_send.at[off], taken_recv.at[off], twin)
-
-    def pass_sum(i, off, to):
-        return remote(kept.at[off], landed.at[i], sum_send.at[i], sum_recv.at[i], to)
-
-    def start(copies):
-        for copy in copies:
-            copy.start()
+    def hop(n, h, place, to, own=False):
+        dst = clips.at[place, core, span(h)]
+        src = tokens_ref.at[span(h)] if own else dst
+        return remote(src, dst, ring_send.at[h, n], ring_recv.at[h, n], to)
+
+    def hop_aux(n, place, to, own=False):
+        dst = aux.at[place, core]
+        src = aux_ref if own else dst
+        return remote(src, dst, ring_send.at[2, n], ring_recv.at[2, n], to)
+
+    def swap(off, h, on, own=False):
+        dst = clips.at[wrap(here + off), on, span(h)]
+        src = tokens_ref.at[span(h)] if own else dst
+        return remote(src, dst, twin_send.at[h, off], twin_recv.at[h, off], twin)
+
+    def swap_aux(off, on, own=False):
+        dst = aux.at[wrap(here + off), on]
+        src = aux_ref if own else dst
+        return remote(src, dst, twin_send.at[2, off], twin_recv.at[2, off], twin)
+
+    def pass_part(off, h):
+        return remote(
+            parts.at[1 - core, off, span(h)],
+            taken.at[off, span(h)],
+            part_send.at[h, off],
+            part_recv.at[h, off],
+            twin,
+        )
+
+    def pass_sum(i, h, off, to):
+        return remote(
+            parts.at[core, off, span(h)],
+            landed.at[i, span(h)],
+            sum_send.at[h, i],
+            sum_recv.at[h, i],
+            to,
+        )
 
     loads = [
         pltpu.make_async_copy(tokens_ref, clips.at[here, core], load_sem.at[0]),
@@ -186,36 +208,40 @@
         pltpu.make_async_copy(up_ref.at[0], up_w, load_sem.at[3]),
         pltpu.make_async_copy(down_ref.at[0], down_w, load_sem.at[4]),
     ]
-    start(loads)
 
     barrier = pltpu.get_barrier_semaphore()
     for other in (ahead, behind, twin):
         pl.semaphore_signal(
             barrier, inc=1, device_id={"block": other}, device_id_type=pl.DeviceIdType.MESH
         )
+    for load in loads:
+        load.start()
     pl.semaphore_wait(barrier, 3)
 
-    loads[0].wait()
-    loads[1].wait()
-    start(hop(1, here, ahead))
-    start(hop(2, here, behind))
-    start(swap(0, core))
-    for load in loads[2:]:
+    for h in range(2):
+        hop(1, h, here, ahead, True).start()
+        hop(2, h, here, behind, True).start()
+        if h == 0:
+            hop_aux(1, here, ahead, True).start()
+            hop_aux(2, here, behind, True).start()
+        swap(0, h, core, True).start()
+    swap_aux(0, core, True).start()
+    for load in loads:
         load.wait()
 
     scale_d = width ** (-0.5)
     scale_m = mem ** (-0.5)
-    eye = lax.broadcasted_iota(jnp.int32, (rows, rows), 0) == lax.broadcasted_iota(
-        jnp.int32, (rows, rows), 1
-    )
-
-    def column(place, on):
-        row = aux[place, on, pl.ds(me, 1), :]
-        return jnp.sum(jnp.where(eye, jnp.broadcast_to(row, (rows, rows)), 0.0), axis=1, keepdims=True)
-
-    def work(off):
-        place = wrap(here + off)
-        x = clips[place].reshape(2 * rows, width)
+    down_row = lax.broadcasted_iota(jnp.int32, (piece, rows), 0)
+    along = lax.broadcasted_iota(jnp.int32, (piece, rows), 1)
+
+    def column(place, on, h):
+        row = jnp.broadcast_to(aux[place, on, pl.ds(me, 1), :], (piece, rows))
+        picked = jnp.where(down_row + h * piece == along, row, 0.0)
+        return jnp.sum(picked, axis=1, keepdims=True)
+
+    def work(halves):
+        pieces = [(off, h, on) for off, h in halves for on in range(2)]
+        x = jnp.concatenate([clips[wrap(here + off), on, span(h), :] for off, h, on in pieces], axis=0)
         hidden = []
         for at in range(0, hidden_width, 256):
             cols = slice(at, min(at + 256, hidden_width))
@@ -223,141 +249,176 @@
             u = dot(x, up_w[:, cols])
             hidden.append((g / (1.0 + jnp.exp(-g)) * u).astype(jnp.bfloat16))
         hidden = jnp.concatenate(hidden, axis=1)
-        shares = jnp.concatenate([column(place, 0), column(place, 1)], axis=0)
+        shares = jnp.concatenate([column(wrap(here + off), on, h) for off, h, on in pieces], axis=0)
         for at in range(0, width, 512):
             cols = slice(at, min(at + 512, width))
             out = (dot(hidden, down_w[:, cols]) * shares).astype(jnp.bfloat16)
-            out = out.reshape(2, rows, out.shape[1])
-
-            @pl.when(core == 0)
-            def _():
-                kept[off, :, cols] = out[0]
-                given[off, :, cols] = out[1]
-
-            @pl.when(core == 1)
-            def _():
-                kept[off, :, cols] = out[1]
-                given[off, :, cols] = out[0]
-
-        pass_part(off).start()
-        scores = (dot(x, keys_ref[...], 1, 1) * scale_d).astype(jnp.bfloat16)
-        for on in range(2):
-            piece = slice(on * rows, (on + 1) * rows)
-            writes[block_of(place, on)] = dot(scores[piece], x[piece], 0, 0) * (1.0 / rows)
-
-    def add_up(off, parts):
-        pass_part(off).wait_recv()
+            for j, (off, h, on) in enumerate(pieces):
+                parts[on, off, span(h), cols] = out[j * piece : (j + 1) * piece]
+        for off, h in halves:
+            pass_part(off, h).start()
+
+    def add_up(off, h, part):
+        pass_part(off, h).wait_recv()
 
         def some(i, _):
-            at = pl.ds(pl.multiple_of(i * 16, 16), 16)
-            total = kept[off, at, :].astype(jnp.float32) + taken[off, at, :].astype(jnp.float32)
-            for part in parts:
+            at = pl.ds(pl.multiple_of(h * piece + i * 16, 16), 16)
+            total = parts[core, off, at, :].astype(jnp.float32)
+            total = total + taken[off, at, :].astype(jnp.float32)
+            if part is not None:
                 total = total + landed[part, at, :].astype(jnp.float32)
-            kept[off, at, :] = total.astype(jnp.bfloat16)
+            parts[core, off, at, :] = total.astype(jnp.bfloat16)
             return 0
 
-        lax.fori_loop(0, rows // 16, some, 0)
-
-    def long_sum(i):
-        off = wrap((half - i) * way)
+        lax.fori_loop(0, piece // 16, some, 0)
+
+    def long_sum(i, h):
+        off = wrap((far - i) * way)
         if i > 0:
-            pass_sum(i - 1, off, ahead).wait_recv()
-        add_up(off, [i - 1] if i > 0 else [])
-        pass_sum(i, off, ahead).start()
-
-    def short_sum(i):
-        off = wrap((i - (half - 1)) * way)
+            pass_sum(i - 1, h, off, ahead).wait_recv()
+        add_up(off, h, i - 1 if i > 0 else None)
+        pass_sum(i, h, off, ahead).start()
+
+    def short_sum(i, h):
+        off = wrap((i - (far - 1)) * way)
         if i > 0:
-            pass_sum(half + i - 1, off, behind).wait_recv()
-        add_up(off, [half + i - 1] if i > 0 else [])
-        pass_sum(half + i, off, behind).start()
-
-    def arrive(n, to):
+            pass_sum(far + i - 1, h, off, behind).wait_recv()
+        add_up(off, h, far + i - 1 if i > 0 else None)
+        pass_sum(far + i, h, off, behind).start()
+
+    def arrive(n, h, to):
         off = offset(n)
         place = wrap(here + off)
-        for copy in hop(n, place, to):
-            copy.wait_recv()
+        hop(n, h, place, to).wait_recv()
 
         @pl.when(n + 2 <= turn - 1)
         def _():
-            start(hop(n + 2, place, to))
-
-        start(swap(off, core))
-
-    def step(n, _):
-        off = offset(n)
-
-        @pl.when(lax.rem(n, 2) == 1)
-        def _():
-            arrive(n, ahead)
-
-            @pl.when(n + 1 <= turn - 2)
+            hop(n + 2, h, place, to).start()
+
+        swap(off, h, core).start()
+
+        @pl.when(h == 0)
+        def _():
+            hop_aux(n, place, to).wait_recv()
+
+            @pl.when(n + 2 <= turn - 1)
             def _():
-                arrive(n + 1, behind)
-
-        for copy in swap(off, 1 - core):
-            copy.wait_recv()
-        work(off)
-
-        @pl.when(n == turn - 2)
-        def _():
-            short_sum(0)
-
+                hop_aux(n + 2, place, to).start()
+
+            swap_aux(off, core).start()
+
+    def met(off, h):
+        swap(off, h, 1 - core).wait_recv()
+
+        @pl.when(h == 0)
+        def _():
+            swap_aux(off, 1 - core).wait_recv()
+
+    def step(t, _):
+        k = (t + 1) // 2
+        edge = (t == 0) | (t == turn - 1)
+        h = lax.rem(t + 1, 2)
+        off_a = wrap(-k * way)
+        off_b = wrap(k * way)
+        h_a = jnp.where(edge, 0, h)
+        h_b = jnp.where(edge, 1, h)
+
+        @pl.when(t == turn - 1)
+        def _():
+            short_sum(0, 1)
+
+        @pl.when(t > 0)
+        def _():
+            arrive(2 * k - 1, h_a, ahead)
+
+            @pl.when(t < turn - 1)
+            def _():
+                arrive(2 * k, h_b, behind)
+
+            @pl.when(t == turn - 1)
+            def _():
+                arrive(2 * k - 1, h_b, ahead)
+
+        @pl.when(t == turn - 2)
+        def _():
+            short_sum(0, 0)
+
+        met(off_a, h_a)
+        met(off_b, h_b)
+        work([(off_a, h_a), (off_b, h_b)])
         return 0
 
     lax.fori_loop(0, turn, step, 0)
-    long_sum(0)
-
-    def lap(clip, carry):
-        place_x = lax.rem(clip // 2, 2)
-        place_z = clip // 4
-        place = place_x * (2 * line - 1 - place_z) + (1 - place_x) * place_z
-        keep = keep_row(aux[place, lax.rem(clip, 2), count:, :])
-        longer = keep * state_ref[...] + writes[clip]
-        state_ref[...] = longer
-        return carry
-
-    def keep_row(block):
+    long_sum(0, 0)
+    long_sum(0, 1)
+
+    def keep_row(clip):
+        block = aux[place_of(clip), lax.rem(clip, 2), count:, :]
         return jnp.concatenate([block[i : i + 1, :] for i in range(block.shape[0])], axis=1)
 
+    def remember(clip):
+        x = clips[place_of(clip), lax.rem(clip, 2)]
+        scores = (dot(x, keys_ref[...], 1, 1) * scale_d).astype(jnp.bfloat16)
+        write = dot(scores, x, 0, 0) * (1.0 / rows)
+        state_ref[...] = keep_row(clip) * state_ref[...] + write
+
+    def lap(clip, _):
+        @pl.when(clip < me)
+        def _():
+            remember(clip)
+
+        return 0
+
+    def recall():
+        read = state_ref[...].astype(jnp.bfloat16)
+        remember(me)
+        scores = (dot(clips[here, core], read, 1, 1) * scale_d).astype(jnp.bfloat16)
+        for at in range(0, width, 512):
+            cols = slice(at, min(at + 512, width))
+            base[:, cols] = dot(scores, read[:, cols]) * scale_m
+
     state_ref[...] = jnp.zeros((mem, width), jnp.float32)
-    lax.fori_loop(0, me, lap, 0)
-    read = state_ref[...].astype(jnp.bfloat16)
-    lap(me, 0)
-    own = clips[here, core]
-    scores = (dot(own, read, 1, 1) * scale_d).astype(jnp.bfloat16)
-    for at in range(0, width, 512):
-        cols = slice(at, min(at + 512, width))
-        base[:, cols] = dot(scores, read[:, cols]) * scale_m
-
-    for i in range(1, half):
-        if i < half - 1:
-            short_sum(i)
-        long_sum(i)
-
-    pass_part(0).wait_recv()
-    pass_sum(half - 1, 0, ahead).wait_recv()
-    pass_sum(2 * half - 2, 0, behind).wait_recv()
-
-    def finish_some(i, _):
-        at = pl.ds(pl.multiple_of(i * 16, 16), 16)
-        total = kept[0, at, :].astype(jnp.float32) + taken[0, at, :].astype(jnp.float32)
-        total = total + landed[half - 1, at, :].astype(jnp.float32)
-        total = total + landed[2 * half - 2, at, :].astype(jnp.float32)
-        mixed_ref[at, :] = (total + base[at, :]).astype(jnp.bfloat16)
-        return 0
-
-    lax.fori_loop(0, rows // 16, finish_some, 0)
+    gaps = 2 * (far - 2)
+    share = -(-count // gaps)
+    gap = 0
+    for i in range(1, far):
+        for h in range(2):
+            if gap < gaps:
+                lax.fori_loop(gap * share, min((gap + 1) * share, count), lap, 0)
+            elif gap == gaps:
+                recall()
+            gap += 1
+            if i < far - 1:
+                short_sum(i, h)
+            long_sum(i, h)
+
+    for h in range(2):
+        pass_part(0, h).wait_recv()
+        pass_sum(2 * far - 2, h, 0, behind).wait_recv()
+        pass_sum(far - 1, h, 0, ahead).wait_recv()
+
+        def finish_some(i, _):
+            at = pl.ds(pl.multiple_of(h * piece + i * 16, 16), 16)
+            total = parts[core, 0, at, :].astype(jnp.float32) + taken[0, at, :].astype(jnp.float32)
+            total = total + landed[far - 1, at, :].astype(jnp.float32)
+            total = total + landed[2 * far - 2, at, :].astype(jnp.float32)
+            mixed_ref[at, :] = (total + base[at, :]).astype(jnp.bfloat16)
+            return 0
+
+        lax.fori_loop(0, piece // 16, finish_some, 0)
 
     for n in range(1, turn):
-        for copy in hop(n, here, ahead):
-            copy.wait_send()
+        hop_aux(n, here, ahead).wait_send()
+        for h in range(2):
+            hop(n, h, here, ahead).wait_send()
     for off in range(turn):
-        for copy in swap(off, core):
-            copy.wait_send()
-        pass_part(off).wait_send()
-    for i in range(2 * half - 1):
-        pass_sum(i, 0, ahead).wait_send()
+        swap_aux(off, core).wait_send()
+        for h in range(2):
+            swap(off, h, core).wait_send()
+            pass_part(off, h).wait_send()
+    for i in range(2 * far - 1):
+        for h in range(2):
+            pass_sum(i, h, 0, ahead).wait_send()
 
 
 def dense(tokens, expert_ids, route_weight, memory_keep, mem_keys, w_gate, w_up, w_down):
@@ -387,21 +448,19 @@
             pltpu.VMEM((width, hidden), bf16),
             pltpu.VMEM((width, hidden), bf16),
             pltpu.VMEM((hidden, width), bf16),
-            pltpu.VMEM((turn, rows, width), bf16),
-            pltpu.VMEM((turn, rows, width), bf16),
+            pltpu.VMEM((2, turn, rows, width), bf16),
             pltpu.VMEM((turn, rows, width), bf16),
             pltpu.VMEM((turn - 1, rows, width), bf16),
-            pltpu.VMEM((count, mem, width), f32),
             pltpu.VMEM((rows, width), f32),
             dma((5,)),
+            dma((3, turn)),
+            dma((3, turn)),
+            dma((3, turn)),
+            dma((3, turn)),
             dma((2, turn)),
             dma((2, turn)),
-            dma((2, turn)),
-            dma((2, turn)),
-            dma((turn,)),
-            dma((turn,)),
-            dma((turn - 1,)),
-            dma((turn - 1,)),
+            dma((2, turn - 1)),
+            dma((2, turn - 1)),
         ],
         compiler_params=pltpu.CompilerParams(
             collective_id=0, has_side_effects=True, vmem_limit_bytes=56 * 2**20

time: 115 us -> 102 us (0.89)
  Pallas kernels: 109 us -> 95.2 us
    pallas_call x1, Pallas kernels: 109 us -> 95.2 us  [dense(): pl.pallas_call(functools.partial(dense_kernel, count), out_shape=(jax.Sha...]
where the time goes in v1:
time: 102 us; the launch traced here: 101 us
  Pallas kernels  95.2 us (93%)
  local copies, waits for them, and re-layouts  3.55 us (3%)
  other arithmetic  2.03 us (2%)
    pallas_call x1, Pallas kernels, dense(): pl.pallas_call(functools.partial(dense_kernel, count), out_shape=(jax.Sha...  95.2 us
    unnamed x2, local copies, waits for them, and re-layouts  3.55 us

profile of v1, /device:TPU:0, one launch (start us, length us, event | category | flops | bytes accessed | tf_op | source)
XLA Modules:
  0.0 101.4 jit_solution(11953027177514802996)
XLA Ops:
  0.6 0.7 select_reduce_fusion
  1.4 1.3 %pad_maximum_fusion.aux_ref = f32[32,128]{1,0:T(8,128)} fusion(f32[16,128]{1,0:T(8,128)} %bitcast.1, f32[16,128]{1,0:T(8,128)S(1)} %select_reduce_fusion), kind=kLoop, calls=%fused_computation.2 | loop fusion | flops 4096 | bytes 32768 | tf_op jit(solution)/shard_map/concatenate | solution.py:432
  2.7 95.2 %shard_map.95 = (bf16[128,2048]{1,0:T(8,128)(2,1)}, f32[32,2048]{1,0:T(8,128)}) custom-call(bf16[128,2048]{1,0:T(8,128)(2,1)} %tokens_ref.1, f32[32,128]{1,0:T(8,128)} %pad_maximum_fusion.aux_ref, bf16[32,2048]{1,0:T(8,128)(2,1)} %keys_ref.1, bf16[1,2048,768]{2,1,0:T(8,128)(2,1)} %gate_ref.1, bf16[1,2048,768]{2,1,0:T(8,128)(2,1)} %up_ref.1, ...), custom_call_target="tpu_custom_call" | custom-call | flops 19327352832 | bytes 9437184 | tf_op jit(solution)/shard_map/pallas_call | solution.py:437
  97.9 1.9 %copy.14 = bf16[128,2048]{1,0:T(8,128)(2,1)} copy(bf16[128,2048]{1,0:T(8,128)(2,1)} %get-tuple-element.4) | data formatting | bytes 1048576
  99.8 1.7 %copy.15 = f32[32,2048]{1,0:T(8,128)} copy(f32[32,2048]{1,0:T(8,128)} %get-tuple-element.5) | data formatting | bytes 524288

commit v2 on v1

--- a/solution.py
+++ b/solution.py
@@ -89,7 +89,9 @@
 def dense_kernel(
     count,
     tokens_ref,
-    aux_ref,
+    ids_ref,
+    weight_ref,
+    keep_ref,
     keys_ref,
     gate_ref,
     up_ref,
@@ -98,6 +100,11 @@
     state_ref,
     clips,
     aux,
+    ids,
+    weight,
+    keys,
+    state,
+    mixed,
     gate_w,
     up_w,
     down_w,
@@ -106,6 +113,7 @@
     landed,
     base,
     load_sem,
+    out_sem,
     ring_send,
     ring_recv,
     twin_send,
@@ -121,7 +129,7 @@
     rows, width = tokens_ref.shape
     piece = rows // 2
     hidden_width = gate_w.shape[1]
-    mem = keys_ref.shape[0]
+    mem = keys.shape[0]
     me = lax.axis_index("block")
     core = lax.rem(me, 2)
     way = 1 - 2 * core
@@ -168,20 +176,18 @@
         src = tokens_ref.at[span(h)] if own else dst
         return remote(src, dst, ring_send.at[h, n], ring_recv.at[h, n], to)
 
-    def hop_aux(n, place, to, own=False):
-        dst = aux.at[place, core]
-        src = aux_ref if own else dst
-        return remote(src, dst, ring_send.at[2, n], ring_recv.at[2, n], to)
+    def hop_aux(n, place, to):
+        both = aux.at[place, core]
+        return remote(both, both, ring_send.at[2, n], ring_recv.at[2, n], to)
 
     def swap(off, h, on, own=False):
         dst = clips.at[wrap(here + off), on, span(h)]
         src = tokens_ref.at[span(h)] if own else dst
         return remote(src, dst, twin_send.at[h, off], twin_recv.at[h, off], twin)
 
-    def swap_aux(off, on, own=False):
-        dst = aux.at[wrap(here + off), on]
-        src = aux_ref if own else dst
-        return remote(src, dst, twin_send.at[2, off], twin_recv.at[2, off], twin)
+    def swap_aux(off, on):
+        both = aux.at[wrap(here + off), on]
+        return remote(both, both, twin_send.at[2, off], twin_recv.at[2, off], twin)
 
     def pass_part(off, h):
         return remote(
@@ -202,11 +208,19 @@
         )
 
     loads = [
-        pltpu.make_async_copy(tokens_ref, clips.at[here, core], load_sem.at[0]),
-        pltpu.make_async_copy(aux_ref, aux.at[here, core], load_sem.at[1]),
-        pltpu.make_async_copy(gate_ref.at[0], gate_w, load_sem.at[2]),
-        pltpu.make_async_copy(up_ref.at[0], up_w, load_sem.at[3]),
-        pltpu.make_async_copy(down_ref.at[0], down_w, load_sem.at[4]),
+        pltpu.make_async_copy(src, dst, load_sem.at[i])
+        for i, (src, dst) in enumerate(
+            (
+                (ids_ref, ids),
+                (weight_ref, weight),
+                (keep_ref, aux.at[here, core, pl.ds(count, width // rows)]),
+                (tokens_ref, clips.at[here, core]),
+                (gate_ref.at[0], gate_w),
+                (up_ref.at[0], up_w),
+                (down_ref.at[0], down_w),
+                (keys_ref, keys),
+            )
+        )
     ]
 
     barrier = pltpu.get_barrier_semaphore()
@@ -221,13 +235,16 @@
     for h in range(2):
         hop(1, h, here, ahead, True).start()
         hop(2, h, here, behind, True).start()
+        swap(0, h, core, True).start()
         if h == 0:
-            hop_aux(1, here, ahead, True).start()
-            hop_aux(2, here, behind, True).start()
-        swap(0, h, core, True).start()
-    swap_aux(0, core, True).start()
-    for load in loads:
-        load.wait()
+            for load in loads[:3]:
+                load.wait()
+            for e in range(count):
+                named = jnp.where(ids[...] == e, weight[...], 0.0)
+                aux[here, core, e : e + 1, :] = jnp.sum(named, axis=0, keepdims=True)
+            hop_aux(1, here, ahead).start()
+            hop_aux(2, here, behind).start()
+            swap_aux(0, core).start()
 
     scale_d = width ** (-0.5)
     scale_m = mem ** (-0.5)
@@ -323,6 +340,11 @@
         h_a = jnp.where(edge, 0, h)
         h_b = jnp.where(edge, 1, h)
 
+        @pl.when(t == 0)
+        def _():
+            for load in loads[3:]:
+                load.wait()
+
         @pl.when(t == turn - 1)
         def _():
             short_sum(0, 1)
@@ -349,8 +371,10 @@
         return 0
 
     lax.fori_loop(0, turn, step, 0)
+    short_sum(1, 0)
     long_sum(0, 0)
     long_sum(0, 1)
+    short_sum(1, 1)
 
     def keep_row(clip):
         block = aux[place_of(clip), lax.rem(clip, 2), count:, :]
@@ -358,9 +382,9 @@
 
     def remember(clip):
         x = clips[place_of(clip), lax.rem(clip, 2)]
-        scores = (dot(x, keys_ref[...], 1, 1) * scale_d).astype(jnp.bfloat16)
+        scores = (dot(x, keys[...], 1, 1) * scale_d).astype(jnp.bfloat16)
         write = dot(scores, x, 0, 0) * (1.0 / rows)
-        state_ref[...] = keep_row(clip) * state_ref[...] + write
+        state[...] = keep_row(clip) * state[...] + write
 
     def lap(clip, _):
         @pl.when(clip < me)
@@ -370,27 +394,34 @@
         return 0
 
     def recall():
-        read = state_ref[...].astype(jnp.bfloat16)
+        read = state[...].astype(jnp.bfloat16)
         remember(me)
         scores = (dot(clips[here, core], read, 1, 1) * scale_d).astype(jnp.bfloat16)
         for at in range(0, width, 512):
             cols = slice(at, min(at + 512, width))
             base[:, cols] = dot(scores, read[:, cols]) * scale_m
 
-    state_ref[...] = jnp.zeros((mem, width), jnp.float32)
+    state[...] = jnp.zeros((mem, width), jnp.float32)
     gaps = 2 * (far - 2)
     share = -(-count // gaps)
-    gap = 0
+
+    def fill(gap):
+        if gap < gaps:
+            lax.fori_loop(gap * share, min((gap + 1) * share, count), lap, 0)
+        elif gap == gaps:
+            recall()
+            pltpu.make_async_copy(state, state_ref, out_sem.at[2]).start()
+
+    fill(0)
     for i in range(1, far):
         for h in range(2):
-            if gap < gaps:
-                lax.fori_loop(gap * share, min((gap + 1) * share, count), lap, 0)
-            elif gap == gaps:
-                recall()
-            gap += 1
-            if i < far - 1:
-                short_sum(i, h)
+            if i < far - 2:
+                short_sum(i + 1, h)
             long_sum(i, h)
+            fill(2 * (i - 1) + h + 1)
+
+    def ready(h):
+        return pltpu.make_async_copy(mixed.at[span(h)], mixed_ref.at[span(h)], out_sem.at[h])
 
     for h in range(2):
         pass_part(0, h).wait_recv()
@@ -402,10 +433,11 @@
             total = parts[core, 0, at, :].astype(jnp.float32) + taken[0, at, :].astype(jnp.float32)
             total = total + landed[far - 1, at, :].astype(jnp.float32)
             total = total + landed[2 * far - 2, at, :].astype(jnp.float32)
-            mixed_ref[at, :] = (total + base[at, :]).astype(jnp.bfloat16)
+            mixed[at, :] = (total + base[at, :]).astype(jnp.bfloat16)
             return 0
 
         lax.fori_loop(0, piece // 16, finish_some, 0)
+        ready(h).start()
 
     for n in range(1, turn):
         hop_aux(n, here, ahead).wait_send()
@@ -419,32 +451,51 @@
     for i in range(2 * far - 1):
         for h in range(2):
             pass_sum(i, h, 0, ahead).wait_send()
+    pltpu.make_async_copy(state, state_ref, out_sem.at[2]).wait()
+    for h in range(2):
+        ready(h).wait()
+
+
+def settle_kernel(mixed_in, state_in, mixed_ref, state_ref, mixed, state, sem):
+    ways = ((mixed_in, mixed, mixed_ref), (state_in, state, state_ref))
+    into = [pltpu.make_async_copy(src, mid, sem.at[0, i]) for i, (src, mid, _) in enumerate(ways)]
+    out = [pltpu.make_async_copy(mid, dst, sem.at[1, i]) for i, (_, mid, dst) in enumerate(ways)]
+    for copy in into:
+        copy.start()
+    for first, second in zip(into, out):
+        first.wait()
+        second.start()
+    for copy in out:
+        copy.wait()
 
 
 def dense(tokens, expert_ids, route_weight, memory_keep, mem_keys, w_gate, w_up, w_down):
     rows, width = tokens.shape
+    topk = expert_ids.shape[1]
     mem = mem_keys.shape[0]
     hidden = w_gate.shape[2]
     count = lax.axis_size("block")
     turn = count // 2
-    hot = expert_ids[None, :, :] == jnp.arange(count, dtype=jnp.int32)[:, None, None]
-    shares = jnp.sum(jnp.where(hot, route_weight[None, :, :], 0.0), axis=2)
-    aux = jnp.concatenate([shares, memory_keep.reshape(-1, rows)], axis=0)
     bf16, f32 = jnp.bfloat16, jnp.float32
     anywhere = pl.BlockSpec(memory_space=pl.ANY)
-    vmem = pl.BlockSpec(memory_space=pltpu.VMEM)
     dma = pltpu.SemaphoreType.DMA
-    return pl.pallas_call(
+    shapes = (
+        jax.ShapeDtypeStruct((rows, width), bf16),
+        jax.ShapeDtypeStruct((mem, width), f32),
+    )
+    results = pl.pallas_call(
         functools.partial(dense_kernel, count),
-        out_shape=(
-            jax.ShapeDtypeStruct((rows, width), bf16),
-            jax.ShapeDtypeStruct((mem, width), f32),
-        ),
-        in_specs=[anywhere, anywhere, vmem, anywhere, anywhere, anywhere],
-        out_specs=(vmem, vmem),
+        out_shape=shapes,
+        in_specs=[anywhere] * 8,
+        out_specs=(anywhere, anywhere),
         scratch_shapes=[
             pltpu.VMEM((turn, 2, rows, width), bf16),
-            pltpu.VMEM((turn, 2) + aux.shape, f32),
+            pltpu.VMEM((turn, 2, count + width // rows, rows), f32),
+            pltpu.VMEM((topk, rows), jnp.int32),
+            pltpu.VMEM((topk, rows), f32),
+            pltpu.VMEM((mem, width), bf16),
+            pltpu.VMEM((mem, width), f32),
+            pltpu.VMEM((rows, width), bf16),
             pltpu.VMEM((width, hidden), bf16),
             pltpu.VMEM((width, hidden), bf16),
             pltpu.VMEM((hidden, width), bf16),
@@ -452,7 +503,8 @@
             pltpu.VMEM((turn, rows, width), bf16),
             pltpu.VMEM((turn - 1, rows, width), bf16),
             pltpu.VMEM((rows, width), f32),
-            dma((5,)),
+            dma((8,)),
+            dma((3,)),
             dma((3, turn)),
             dma((3, turn)),
             dma((3, turn)),
@@ -468,7 +520,23 @@
         cost_estimate=pl.CostEstimate(
             flops=6 * count * rows * width * hidden, bytes_accessed=2 * 3 * width * hidden, transcendentals=0
         ),
-    )(tokens, aux, mem_keys, w_gate, w_up, w_down)
+    )(
+        tokens,
+        expert_ids.T,
+        route_weight.T,
+        memory_keep.reshape(-1, rows),
+        mem_keys,
+        w_gate,
+        w_up,
+        w_down,
+    )
+    return pl.pallas_call(
+        settle_kernel,
+        out_shape=shapes,
+        in_specs=[anywhere] * 2,
+        out_specs=(anywhere, anywhere),
+        scratch_shapes=[pltpu.VMEM((rows, width), bf16), pltpu.VMEM((mem, width), f32), dma((2, 2))],
+    )(*results)
 
 
 def solution(mesh):

time: 102 us -> 95.2 us (0.933)
  local copies, waits for them, and re-layouts: 3.55 us -> 0 us
  other arithmetic: 2.03 us -> 0 us
    unnamed x2 -> x0, local copies, waits for them, and re-layouts: 3.55 us -> none
    concatenate x1 -> x0, other arithmetic: 1.31 us -> none  [dense(): aux = jnp.concatenate([shares, memory_keep.reshape(-1, rows)], axis=0)]
    pallas_call x1 -> x2, Pallas kernels: 95.2 us -> 94.4 us  [the longest x1 92.5 us: dense(): pl.pallas_call(functools.partial(dense_kernel, count), out_shape=shapes,...]
where the time goes in v2:
time: 95.2 us; the launch traced here: 95.1 us
  Pallas kernels  94.4 us (99%)
    pallas_call x1, Pallas kernels, dense(): pl.pallas_call(functools.partial(dense_kernel, count), out_shape=shapes,...  92.5 us
    pallas_call x1, Pallas kernels, dense(): pl.pallas_call(settle_kernel, out_shape=shapes, in_specs=[anywhere] * 2,...  1.95 us

profile of v2, /device:TPU:0, one launch (start us, length us, event | category | flops | bytes accessed | tf_op | source)
XLA Modules:
  0.0 95.1 jit_solution(17284451460092135442)
XLA Ops:
  0.6 92.5 %shard_map.95 = (bf16[128,2048]{1,0:T(8,128)(2,1)}, f32[32,2048]{1,0:T(8,128)}) custom-call(bf16[128,2048]{1,0:T(8,128)(2,1)} %tokens_ref.1, s32[8,128]{1,0:T(8,128)} %bitcast.4, f32[8,128]{1,0:T(8,128)} %bitcast.5, f32[16,128]{1,0:T(8,128)} %bitcast.3, bf16[32,2048]{1,0:T(8,128)(2,1)} %keys_ref.1, bf16[1,2048,768]{2,1,0:T(8,128)(2,1)} %gate_ref.1, ...), custom_call_target="tpu_custom_call" | custom-call | flops 19327352832 | bytes 9437184 | tf_op jit(solution)/shard_map/pallas_call | solution.py:486
  93.1 2.0 %shard_map.96 = (bf16[128,2048]{1,0:T(8,128)(2,1)}, f32[32,2048]{1,0:T(8,128)}) custom-call(bf16[128,2048]{1,0:T(8,128)(2,1)} %get-tuple-element.4.mixed_in, f32[32,2048]{1,0:T(8,128)} %get-tuple-element.5.state_in), custom_call_target="tpu_custom_call" | custom-call | tf_op jit(solution)/shard_map/pallas_call | solution.py:533

commit v3 on v2

--- a/solution.py
+++ b/solution.py
@@ -128,11 +128,11 @@
     far = turn // 2
     rows, width = tokens_ref.shape
     piece = rows // 2
+    part = piece // 2
     hidden_width = gate_w.shape[1]
     mem = keys.shape[0]
     me = lax.axis_index("block")
     core = lax.rem(me, 2)
-    way = 1 - 2 * core
 
     def place_of(block):
         x = lax.rem(block // 2, 2)
@@ -148,8 +148,9 @@
         return lax.rem(value + 2 * turn, turn)
 
     here = place_of(me)
-    ahead = block_of(wrap(here + way), core)
-    behind = block_of(wrap(here - way), core)
+    ahead = block_of(wrap(here + 1), core)
+    behind = block_of(wrap(here - 1), core)
+    toward = (ahead, behind)
     twin = block_of(here, 1 - core)
 
     def span(h):
@@ -167,18 +168,15 @@
             device_id_type=pl.DeviceIdType.MESH,
         )
 
-    def offset(n):
-        odd = lax.rem(n, 2)
-        return wrap((1 - 2 * odd) * ((n + 1) // 2) * way)
-
-    def hop(n, h, place, to, own=False):
+    def hop(d, k, s, place, own=False):
+        h = (d + s) % 2 if isinstance(s, int) else lax.rem(d + s, 2)
         dst = clips.at[place, core, span(h)]
         src = tokens_ref.at[span(h)] if own else dst
-        return remote(src, dst, ring_send.at[h, n], ring_recv.at[h, n], to)
-
-    def hop_aux(n, place, to):
+        return remote(src, dst, ring_send.at[d, s, k], ring_recv.at[d, s, k], toward[d])
+
+    def hop_aux(d, k, place):
         both = aux.at[place, core]
-        return remote(both, both, ring_send.at[2, n], ring_recv.at[2, n], to)
+        return remote(both, both, ring_send.at[d, 2, k], ring_recv.at[d, 2, k], toward[d])
 
     def swap(off, h, on, own=False):
         dst = clips.at[wrap(here + off), on, span(h)]
@@ -198,13 +196,14 @@
             twin,
         )
 
-    def pass_sum(i, h, off, to):
+    def pass_sum(d, i, h, q):
+        at = pl.ds(h * piece + q * part, part)
         return remote(
-            parts.at[core, off, span(h)],
-            landed.at[i, span(h)],
-            sum_send.at[h, i],
-            sum_recv.at[h, i],
-            to,
+            parts.at[core, wrap((1 - 2 * d) * (far - i)), at],
+            landed.at[d * far + i, at],
+            sum_send.at[d, i, 2 * h + q],
+            sum_recv.at[d, i, 2 * h + q],
+            toward[d],
         )
 
     loads = [
@@ -232,18 +231,18 @@
         load.start()
     pl.semaphore_wait(barrier, 3)
 
-    for h in range(2):
-        hop(1, h, here, ahead, True).start()
-        hop(2, h, here, behind, True).start()
-        swap(0, h, core, True).start()
-        if h == 0:
+    for s in range(2):
+        for d in range(2):
+            hop(d, 1, s, here, True).start()
+        swap(0, s, core, True).start()
+        if s == 0:
             for load in loads[:3]:
                 load.wait()
             for e in range(count):
                 named = jnp.where(ids[...] == e, weight[...], 0.0)
                 aux[here, core, e : e + 1, :] = jnp.sum(named, axis=0, keepdims=True)
-            hop_aux(1, here, ahead).start()
-            hop_aux(2, here, behind).start()
+            for d in range(2):
+                hop_aux(d, 1, here).start()
             swap_aux(0, core).start()
 
     scale_d = width ** (-0.5)
@@ -275,106 +274,95 @@
         for off, h in halves:
             pass_part(off, h).start()
 
-    def add_up(off, h, part):
-        pass_part(off, h).wait_recv()
-
+    def add_up(off, h, q, addends, place):
         def some(i, _):
-            at = pl.ds(pl.multiple_of(h * piece + i * 16, 16), 16)
+            at = pl.ds(pl.multiple_of(h * piece + q * part + i * 16, 16), 16)
             total = parts[core, off, at, :].astype(jnp.float32)
             total = total + taken[off, at, :].astype(jnp.float32)
-            if part is not None:
-                total = total + landed[part, at, :].astype(jnp.float32)
-            parts[core, off, at, :] = total.astype(jnp.bfloat16)
+            for addend in addends:
+                total = total + landed[addend, at, :].astype(jnp.float32)
+            place(off, at, total)
             return 0
 
-        lax.fori_loop(0, piece // 16, some, 0)
-
-    def long_sum(i, h):
-        off = wrap((far - i) * way)
-        if i > 0:
-            pass_sum(i - 1, h, off, ahead).wait_recv()
-        add_up(off, h, i - 1 if i > 0 else None)
-        pass_sum(i, h, off, ahead).start()
-
-    def short_sum(i, h):
-        off = wrap((i - (far - 1)) * way)
-        if i > 0:
-            pass_sum(far + i - 1, h, off, behind).wait_recv()
-        add_up(off, h, far + i - 1 if i > 0 else None)
-        pass_sum(far + i, h, off, behind).start()
-
-    def arrive(n, h, to):
-        off = offset(n)
+        lax.fori_loop(0, part // 16, some, 0)
+
+    def put(off, at, total):
+        parts[core, off, at, :] = total.astype(jnp.bfloat16)
+
+    def pass_on(i, first):
+        for d in range(2):
+            h = d if first else 1 - d
+            off = wrap((1 - 2 * d) * (far - i))
+            more = i > (0 if first else 1)
+            pass_part(off, h).wait_recv()
+            for q in range(2):
+                if more:
+                    pass_sum(d, i - 1, h, q).wait_recv()
+                add_up(off, h, q, [d * far + i - 1] if more else [], put)
+                pass_sum(d, i, h, q).start()
+
+    def arrive(d, k, s):
+        off = wrap((2 * d - 1) * k)
         place = wrap(here + off)
-        hop(n, h, place, to).wait_recv()
-
-        @pl.when(n + 2 <= turn - 1)
-        def _():
-            hop(n + 2, h, place, to).start()
+        h = lax.rem(d + s, 2)
+        hop(d, k, s, place).wait_recv()
+
+        @pl.when((k < far - 1) | ((k == far - 1) & (s == 0)))
+        def _():
+            hop(d, k + 1, s, place).start()
 
         swap(off, h, core).start()
 
-        @pl.when(h == 0)
-        def _():
-            hop_aux(n, place, to).wait_recv()
-
-            @pl.when(n + 2 <= turn - 1)
+        @pl.when((s == 0) & (k < far + 1 - d))
+        def _():
+            hop_aux(d, k, place).wait_recv()
+
+            @pl.when(k < far - d)
             def _():
-                hop_aux(n + 2, place, to).start()
+                hop_aux(d, k + 1, place).start()
 
             swap_aux(off, core).start()
-
-    def met(off, h):
-        swap(off, h, 1 - core).wait_recv()
-
-        @pl.when(h == 0)
-        def _():
-            swap_aux(off, 1 - core).wait_recv()
 
     def step(t, _):
         k = (t + 1) // 2
-        edge = (t == 0) | (t == turn - 1)
-        h = lax.rem(t + 1, 2)
-        off_a = wrap(-k * way)
-        off_b = wrap(k * way)
-        h_a = jnp.where(edge, 0, h)
-        h_b = jnp.where(edge, 1, h)
+        s = lax.rem(t + 1, 2)
+        off_a = wrap(-k)
+        off_b = wrap(k)
 
         @pl.when(t == 0)
         def _():
             for load in loads[3:]:
                 load.wait()
 
+        @pl.when(t > 0)
+        def _():
+            arrive(0, k, s)
+            arrive(1, k, s)
+
+        @pl.when(t == turn - 2)
+        def _():
+            pass_on(1, False)
+
         @pl.when(t == turn - 1)
         def _():
-            short_sum(0, 1)
-
-        @pl.when(t > 0)
-        def _():
-            arrive(2 * k - 1, h_a, ahead)
-
-            @pl.when(t < turn - 1)
-            def _():
-                arrive(2 * k, h_b, behind)
-
-            @pl.when(t == turn - 1)
-            def _():
-                arrive(2 * k - 1, h_b, ahead)
-
-        @pl.when(t == turn - 2)
-        def _():
-            short_sum(0, 0)
-
-        met(off_a, h_a)
-        met(off_b, h_b)
-        work([(off_a, h_a), (off_b, h_b)])
+            pass_on(2, False)
+
+        swap(off_a, s, 1 - core).wait_recv()
+        swap(off_b, 1 - s, 1 - core).wait_recv()
+
+        @pl.when((s == 0) | (t == 0))
+        def _():
+            swap_aux(off_a, 1 - core).wait_recv()
+
+        @pl.when((s == 0) & (k < far))
+        def _():
+            swap_aux(off_b, 1 - core).wait_recv()
+
+        work([(off_a, s), (off_b, 1 - s)])
         return 0
 
     lax.fori_loop(0, turn, step, 0)
-    short_sum(1, 0)
-    long_sum(0, 0)
-    long_sum(0, 1)
-    short_sum(1, 1)
+    pass_on(0, True)
 
     def keep_row(clip):
         block = aux[place_of(clip), lax.rem(clip, 2), count:, :]
@@ -402,55 +390,48 @@
             base[:, cols] = dot(scores, read[:, cols]) * scale_m
 
     state[...] = jnp.zeros((mem, width), jnp.float32)
-    gaps = 2 * (far - 2)
-    share = -(-count // gaps)
-
-    def fill(gap):
-        if gap < gaps:
-            lax.fori_loop(gap * share, min((gap + 1) * share, count), lap, 0)
-        elif gap == gaps:
+    share = -(-count // (far - 2))
+    for i in range(1, far):
+        if i < far - 1:
+            lax.fori_loop((i - 1) * share, min(i * share, count), lap, 0)
+        else:
             recall()
             pltpu.make_async_copy(state, state_ref, out_sem.at[2]).start()
-
-    fill(0)
-    for i in range(1, far):
-        for h in range(2):
-            if i < far - 2:
-                short_sum(i + 1, h)
-            long_sum(i, h)
-            fill(2 * (i - 1) + h + 1)
+        pass_on(i, True)
+        if 2 < i + 2 < far:
+            pass_on(i + 2, False)
 
     def ready(h):
         return pltpu.make_async_copy(mixed.at[span(h)], mixed_ref.at[span(h)], out_sem.at[h])
 
+    def finish_some(off, at, total):
+        mixed[at, :] = (total + base[at, :]).astype(jnp.bfloat16)
+
     for h in range(2):
         pass_part(0, h).wait_recv()
-        pass_sum(2 * far - 2, h, 0, behind).wait_recv()
-        pass_sum(far - 1, h, 0, ahead).wait_recv()
-
-        def finish_some(i, _):
-            at = pl.ds(pl.multiple_of(h * piece + i * 16, 16), 16)
-            total = parts[core, 0, at, :].astype(jnp.float32) + taken[0, at, :].astype(jnp.float32)
-            total = total + landed[far - 1, at, :].astype(jnp.float32)
-            total = total + landed[2 * far - 2, at, :].astype(jnp.float32)
-            mixed[at, :] = (total + base[at, :]).astype(jnp.bfloat16)
-            return 0
-
-        lax.fori_loop(0, piece // 16, finish_some, 0)
+        for q in range(2):
+            for d in range(2):
+                pass_sum(d, far - 1, h, q).wait_recv()
+            add_up(0, h, q, [far - 1, 2 * far - 1], finish_some)
         ready(h).start()
 
-    for n in range(1, turn):
-        hop_aux(n, here, ahead).wait_send()
-        for h in range(2):
-            hop(n, h, here, ahead).wait_send()
+    for d in range(2):
+        for k in range(1, far + 1):
+            if k < far + 1 - d:
+                hop_aux(d, k, here).wait_send()
+            for s in range(2 if k < far else 1):
+                hop(d, k, s, here).wait_send()
     for off in range(turn):
         swap_aux(off, core).wait_send()
         for h in range(2):
             swap(off, h, core).wait_send()
             pass_part(off, h).wait_send()
-    for i in range(2 * far - 1):
-        for h in range(2):
-            pass_sum(i, h, 0, ahead).wait_send()
+    for d in range(2):
+        for i in range(far):
+            for h in range(2):
+                if i > 0 or h == d:
+                    for q in range(2):
+                        pass_sum(d, i, h, q).wait_send()
     pltpu.make_async_copy(state, state_ref, out_sem.at[2]).wait()
     for h in range(2):
         ready(h).wait()
@@ -476,6 +457,7 @@
     hidden = w_gate.shape[2]
     count = lax.axis_size("block")
     turn = count // 2
+    far = turn // 2
     bf16, f32 = jnp.bfloat16, jnp.float32
     anywhere = pl.BlockSpec(memory_space=pl.ANY)
     dma = pltpu.SemaphoreType.DMA
@@ -501,18 +483,18 @@
             pltpu.VMEM((hidden, width), bf16),
             pltpu.VMEM((2, turn, rows, width), bf16),
             pltpu.VMEM((turn, rows, width), bf16),
-            pltpu.VMEM((turn - 1, rows, width), bf16),
+            pltpu.VMEM((turn, rows, width), bf16),
             pltpu.VMEM((rows, width), f32),
             dma((8,)),
             dma((3,)),
-            dma((3, turn)),
-            dma((3, turn)),
+            dma((2, 3, far + 1)),
+            dma((2, 3, far + 1)),
             dma((3, turn)),
             dma((3, turn)),
             dma((2, turn)),
             dma((2, turn)),
-            dma((2, turn - 1)),
-            dma((2, turn - 1)),
+            dma((2, far, 4)),
+            dma((2, far, 4)),
         ],
         compiler_params=pltpu.CompilerParams(
             collective_id=0, has_side_effects=True, vmem_limit_bytes=56 * 2**20

time: 95.2 us -> 93.9 us (0.986)
  Pallas kernels: 94.4 us -> 93.1 us
    pallas_call x1, Pallas kernels: 92.5 us -> 91.2 us  [dense(): pl.pallas_call(functools.partial(dense_kernel, count), out_shape=shapes,...]
where the time goes in v3:
time: 93.9 us; the launch traced here: 93.8 us
  Pallas kernels  93.1 us (99%)
    pallas_call x1, Pallas kernels, dense(): pl.pallas_call(functools.partial(dense_kernel, count), out_shape=shapes,...  91.2 us
    pallas_call x1, Pallas kernels, dense(): pl.pallas_call(settle_kernel, out_shape=shapes, in_specs=[anywhere] * 2,...  1.95 us

profile of v3, /device:TPU:0, one launch (start us, length us, event | category | flops | bytes accessed | tf_op | source)
XLA Modules:
  0.0 93.8 jit_solution(11973355459244184732)
XLA Ops:
  0.6 91.2 %shard_map.95 = (bf16[128,2048]{1,0:T(8,128)(2,1)}, f32[32,2048]{1,0:T(8,128)}) custom-call(bf16[128,2048]{1,0:T(8,128)(2,1)} %tokens_ref.1, s32[8,128]{1,0:T(8,128)} %bitcast.4, f32[8,128]{1,0:T(8,128)} %bitcast.5, f32[16,128]{1,0:T(8,128)} %bitcast.3, bf16[32,2048]{1,0:T(8,128)(2,1)} %keys_ref.1, bf16[1,2048,768]{2,1,0:T(8,128)(2,1)} %gate_ref.1, ...), custom_call_target="tpu_custom_call" | custom-call | flops 19327352832 | bytes 9437184 | tf_op jit(solution)/shard_map/pallas_call | solution.py:468
  91.8 2.0 %shard_map.96 = (bf16[128,2048]{1,0:T(8,128)(2,1)}, f32[32,2048]{1,0:T(8,128)}) custom-call(bf16[128,2048]{1,0:T(8,128)(2,1)} %get-tuple-element.4.mixed_in, f32[32,2048]{1,0:T(8,128)} %get-tuple-element.5.state_in), custom_call_target="tpu_custom_call" | custom-call | tf_op jit(solution)/shard_map/pallas_call | solution.py:515

commit v4 on v3

--- a/solution.py
+++ b/solution.py
@@ -123,12 +123,13 @@
     sum_send,
     sum_recv,
 ):
+    cuts = 4
     turn = count // 2
     line = turn // 2
     far = turn // 2
     rows, width = tokens_ref.shape
     piece = rows // 2
-    part = piece // 2
+    part = piece // cuts
     hidden_width = gate_w.shape[1]
     mem = keys.shape[0]
     me = lax.axis_index("block")
@@ -201,8 +202,8 @@
         return remote(
             parts.at[core, wrap((1 - 2 * d) * (far - i)), at],
             landed.at[d * far + i, at],
-            sum_send.at[d, i, 2 * h + q],
-            sum_recv.at[d, i, 2 * h + q],
+            sum_send.at[d, i, cuts * h + q],
+            sum_recv.at[d, i, cuts * h + q],
             toward[d],
         )
 
@@ -295,7 +296,7 @@
             off = wrap((1 - 2 * d) * (far - i))
             more = i > (0 if first else 1)
             pass_part(off, h).wait_recv()
-            for q in range(2):
+            for q in range(cuts):
                 if more:
                     pass_sum(d, i - 1, h, q).wait_recv()
                 add_up(off, h, q, [d * far + i - 1] if more else [], put)
@@ -334,14 +335,14 @@
             for load in loads[3:]:
                 load.wait()
 
+        @pl.when(t == turn - 2)
+        def _():
+            pass_on(1, False)
+
         @pl.when(t > 0)
         def _():
             arrive(0, k, s)
             arrive(1, k, s)
-
-        @pl.when(t == turn - 2)
-        def _():
-            pass_on(1, False)
 
         @pl.when(t == turn - 1)
         def _():
@@ -409,7 +410,7 @@
 
     for h in range(2):
         pass_part(0, h).wait_recv()
-        for q in range(2):
+        for q in range(cuts):
             for d in range(2):
                 pass_sum(d, far - 1, h, q).wait_recv()
             add_up(0, h, q, [far - 1, 2 * far - 1], finish_some)
@@ -430,7 +431,7 @@
         for i in range(far):
             for h in range(2):
                 if i > 0 or h == d:
-                    for q in range(2):
+                    for q in range(cuts):
                         pass_sum(d, i, h, q).wait_send()
     pltpu.make_async_copy(state, state_ref, out_sem.at[2]).wait()
     for h in range(2):
@@ -493,8 +494,8 @@
             dma((3, turn)),
             dma((2, turn)),
             dma((2, turn)),
-            dma((2, far, 4)),
-            dma((2, far, 4)),
+            dma((2, far, 8)),
+            dma((2, far, 8)),
         ],
         compiler_params=pltpu.CompilerParams(
             collective_id=0, has_side_effects=True, vmem_limit_bytes=56 * 2**20

time: 93.9 us -> 93.3 us (level)
  Pallas kernels: 93.1 us -> 92.1 us
    pallas_call x1, Pallas kernels: 91.2 us -> 90.2 us  [dense(): pl.pallas_call(functools.partial(dense_kernel, count), out_shape=shapes,...]
where the time goes in v4:
time: 93.3 us; the launch traced here: 92.8 us
  Pallas kernels  92.1 us (99%)
    pallas_call x1, Pallas kernels, dense(): pl.pallas_call(functools.partial(dense_kernel, count), out_shape=shapes,...  90.2 us
    pallas_call x1, Pallas kernels, dense(): pl.pallas_call(settle_kernel, out_shape=shapes, in_specs=[anywhere] * 2,...  1.95 us

profile of v4, /device:TPU:0, one launch (start us, length us, event | category | flops | bytes accessed | tf_op | source)
XLA Modules:
  0.0 92.8 jit_solution(9260694802457396213)
XLA Ops:
  0.6 90.2 %shard_map.95 = (bf16[128,2048]{1,0:T(8,128)(2,1)}, f32[32,2048]{1,0:T(8,128)}) custom-call(bf16[128,2048]{1,0:T(8,128)(2,1)} %tokens_ref.1, s32[8,128]{1,0:T(8,128)} %bitcast.4, f32[8,128]{1,0:T(8,128)} %bitcast.5, f32[16,128]{1,0:T(8,128)} %bitcast.3, bf16[32,2048]{1,0:T(8,128)(2,1)} %keys_ref.1, bf16[1,2048,768]{2,1,0:T(8,128)(2,1)} %gate_ref.1, ...), custom_call_target="tpu_custom_call" | custom-call | flops 19327352832 | bytes 9437184 | tf_op jit(solution)/shard_map/pallas_call | solution.py:469
  90.8 2.0 %shard_map.96 = (bf16[128,2048]{1,0:T(8,128)(2,1)}, f32[32,2048]{1,0:T(8,128)}) custom-call(bf16[128,2048]{1,0:T(8,128)(2,1)} %get-tuple-element.4.mixed_in, f32[32,2048]{1,0:T(8,128)} %get-tuple-element.5.state_in), custom_call_target="tpu_custom_call" | custom-call | tf_op jit(solution)/shard_map/pallas_call | solution.py:516
